TPU v7x, 32 devices: a whole 2x2x4 slice. The times are simulated.
32 devices in a mesh: pipe: 2 (over x), expert: 16 (over z, y, core).
Axes of the slice: x: 2, y: 2, z: 4, core: 2. Of those that a mesh axis runs over, the one named last changes fastest.
Arguments:
- down_tokens: bfloat16 [2, 512, 3584], P(None, 'expert'), may hold values from -6 to 6
- up_tokens: bfloat16 [2, 512, 3584], P(None, 'expert'), may hold values from -6 to 6
- norm_gain: float32 [2, 3584], P('pipe'), may hold values from 0.1 to 1.9
- w_gate: bfloat16 [2, 16, 3584, 1024], P('pipe', 'expert'), may hold values from -0.09375 to 0.09375
- w_up: bfloat16 [2, 16, 3584, 1024], P('pipe', 'expert'), may hold values from -0.09375 to 0.09375
- w_down: bfloat16 [2, 16, 1024, 3584], P('pipe', 'expert'), may hold values from -0.1875 to 0.1875
- down_ids: int32 [2, 2, 512, 8], P('pipe', None, 'expert'), may hold values from 0 to 15, all different within a row; in each aligned block of 32 rows (0 to 31, 32 to 63, ..., all dimensions but the last counted through in order) at most 20 rows name the same one
- down_gates: float32 [2, 2, 512, 8], P('pipe', None, 'expert'), may hold values from 0.1 to 1
- up_ids: int32 [2, 2, 512, 8], P('pipe', None, 'expert'), may hold values from 0 to 15, all different within a row; in each aligned block of 32 rows (0 to 31, 32 to 63, ..., all dimensions but the last counted through in order) at most 20 rows name the same one
- up_gates: float32 [2, 2, 512, 8], P('pipe', None, 'expert'), may hold values from 0.1 to 1
- key_cotangent: bfloat16 [2, 2, 2, 512, 64], P('pipe', None, None, 'expert'), may hold values from -0.119628906 to 0.119628906
Outputs:
- down_states: bfloat16 [2, 2, 512, 3584], P('pipe', None, 'expert')
- up_states: bfloat16 [2, 2, 512, 3584], P('pipe', None, 'expert')
- kr_grad: float32 [2, 3584, 64], P('pipe', 'expert')
Inputs may be any that keep to these rules, and one draw needn't show every extreme that they name: `down_ids`: each row names 8 different experts. Among the 32 rows of one device in one micro-batch at one section, no expert is named more than 20 times, a bound that some block reaches. `up_ids`: each row names 8 different experts. Among the 32 rows of one device in one micro-batch at one section, no expert is named more than 20 times, a bound that some block reaches.
All inputs are finite; a program needn't handle non-finite values.
Results may differ from a plain program's by a relative error of at most 0.017.
Values may be sent and summed in bfloat16 or wider, within the bound.
A program may use at most 128 MiB of HBM per device.

v0:
```python
from functools import partial

import jax
import jax.numpy as jnp
from jax import lax
from jax.sharding import PartitionSpec as P

EPSILON = 1e-06


def passed_along(value, axis, steps):
    count = lax.axis_size(axis)
    first, last = (max(0, -steps), min(count, count - steps))
    return lax.ppermute(value, axis, [(source, source + steps) for source in range(first, last)])


def normalize(carried, norm_scale):
    values = carried.astype(jnp.float32)
    inv_rms = lax.rsqrt(jnp.mean(values * values, axis=-1, keepdims=True) + EPSILON)
    return (values * inv_rms * norm_scale).astype(jnp.bfloat16)


def expert_rows(row_block, gate_mat, up_mat, down_mat):
    gate_act = jnp.dot(row_block, gate_mat, preferred_element_type=jnp.float32)
    up_act = jnp.dot(row_block, up_mat, preferred_element_type=jnp.float32)
    hidden = (jax.nn.silu(gate_act) * up_act).astype(jnp.bfloat16)
    return jnp.dot(hidden, down_mat, preferred_element_type=jnp.float32).astype(jnp.bfloat16)


def apply_expert(row_block, weights):
    return expert_rows(row_block, weights[0], weights[1], weights[2])


def slot_layout(route_ids, expert_count, capacity):
    expert_axis = jnp.arange(expert_count, dtype=jnp.int32)
    chosen = jnp.sum((route_ids[:, :, None] == expert_axis).astype(jnp.int32), axis=1)
    slot_rank = jnp.cumsum(chosen, axis=0) - 1
    slot_axis = jnp.arange(capacity, dtype=jnp.int32)
    return chosen[:, :, None] * (slot_rank[:, :, None] == slot_axis).astype(jnp.int32)


def run_layer(carried, norm_scale, weights, route_ids, route_gates, active):
    normed = normalize(carried, norm_scale)
    expert_count = lax.axis_size("expert")
    token_count, pick_count = route_ids.shape
    capacity = min(token_count, 5 * token_count * pick_count // (4 * expert_count))
    slot_table = slot_layout(route_ids, expert_count, capacity)
    outgoing = jnp.einsum(
        "tec,td->ecd", slot_table.astype(jnp.bfloat16), normed, preferred_element_type=jnp.float32
    ).astype(jnp.bfloat16)
    arrived = lax.all_to_all(outgoing, "expert", split_axis=0, concat_axis=0, tiled=True)
    source_count, item_count, feature_count = arrived.shape
    row_block = arrived.reshape(source_count * item_count, feature_count)
    finished = lax.cond(active, partial(apply_expert, weights=weights), jnp.zeros_like, row_block)
    returned = lax.all_to_all(
        finished.reshape(source_count, item_count, feature_count),
        "expert",
        split_axis=0,
        concat_axis=0,
        tiled=True,
    )
    expert_axis = jnp.arange(expert_count, dtype=jnp.int32)
    gate_weight = jnp.sum(
        route_gates[:, :, None] * (route_ids[:, :, None] == expert_axis).astype(jnp.float32), axis=1
    )
    weighted = (slot_table.astype(jnp.float32) * gate_weight[:, :, None]).reshape(
        token_count, expert_count * capacity
    )
    flat_returned = returned.reshape(expert_count * capacity, returned.shape[2]).astype(jnp.float32)
    combined = jnp.dot(weighted, flat_returned, precision=lax.Precision.HIGHEST)
    output = (carried.astype(jnp.float32) + combined).astype(jnp.bfloat16)
    return (output, normed)


def pass_on(values):
    to_next = passed_along(values, "pipe", 1)
    behind = passed_along(values, "pipe", -1)
    return (to_next, behind)


def grad_term(row_source, tangents):
    return jnp.einsum("td,tr->dr", row_source, tangents, preferred_element_type=jnp.float32)


def on_device(
    down_tokens,
    up_tokens,
    norm_gain,
    w_gate,
    w_up,
    w_down,
    down_ids,
    down_gates,
    up_ids,
    up_gates,
    key_cotangent,
):
    segment_count = lax.axis_size("pipe")
    segment_pos = lax.axis_index("pipe")
    micro_count = down_tokens.shape[0]
    norm_scale = norm_gain[0]
    weights = (w_gate[0, 0], w_up[0, 0], w_down[0, 0])
    total_steps = segment_count + 2 * micro_count - 2
    from_prior = jnp.zeros_like(down_tokens[0])
    from_next = jnp.zeros_like(up_tokens[0])
    down_states = jnp.zeros_like(down_tokens)
    up_states = jnp.zeros_like(up_tokens)
    saved_rows = []
    saved_tangents = []
    micro_slots = jnp.arange(micro_count, dtype=jnp.int32)
    for step_index in range(total_steps):
        lag_down = step_index - segment_pos
        lag_up = step_index - (segment_count - 1 - segment_pos)
        down_on = (lag_down >= 0) & (lag_down % 2 == 0) & (lag_down < 2 * micro_count)
        up_on = (lag_up >= 0) & (lag_up % 2 == 0) & (lag_up < 2 * micro_count)
        down_mb = jnp.clip(lag_down // 2, 0, micro_count - 1)
        up_mb = jnp.clip(lag_up // 2, 0, micro_count - 1)
        down_in = jnp.where(segment_pos == 0, down_tokens[down_mb], from_prior)
        up_in = jnp.where(segment_pos == segment_count - 1, up_tokens[up_mb], from_next)
        carried = jnp.where(down_on, down_in, up_in)
        route_ids = jnp.where(down_on, down_ids[0, down_mb], up_ids[0, up_mb])
        route_gates = jnp.where(down_on, down_gates[0, down_mb], up_gates[0, up_mb])
        active = down_on | up_on
        output, normed = run_layer(carried, norm_scale, weights, route_ids, route_gates, active)
        down_states = jnp.where(
            (micro_slots == down_mb)[:, None, None] & down_on, output[None], down_states
        )
        up_states = jnp.where(
            (micro_slots == up_mb)[:, None, None] & up_on, output[None], up_states
        )
        tangent = jnp.where(down_on, key_cotangent[0, 0, down_mb], key_cotangent[0, 1, up_mb])
        tangent = tangent * active.astype(tangent.dtype)
        saved_rows.append(normed)
        saved_tangents.append(tangent)
        if step_index + 1 < total_steps:
            from_prior, from_next = pass_on(output)
    all_rows_kept = jnp.concatenate(saved_rows, axis=0)
    all_tangents = jnp.concatenate(saved_tangents, axis=0)
    key_grad_acc = lax.psum_scatter(
        grad_term(all_rows_kept, all_tangents).astype(jnp.bfloat16),
        "expert",
        scatter_dimension=0,
        tiled=True,
    ).astype(jnp.float32)
    return (down_states[None], up_states[None], key_grad_acc[None])


def solution(mesh):
    return jax.shard_map(
        on_device,
        mesh=mesh,
        in_specs=(
            P(None, "expert", None),
            P(None, "expert", None),
            P("pipe", None),
            P("pipe", "expert", None, None),
            P("pipe", "expert", None, None),
            P("pipe", "expert", None, None),
            P("pipe", None, "expert", None),
            P("pipe", None, "expert", None),
            P("pipe", None, "expert", None),
            P("pipe", None, "expert", None),
            P("pipe", None, None, "expert", None),
        ),
        out_specs=(
            P("pipe", None, "expert", None),
            P("pipe", None, "expert", None),
            P("pipe", "expert", None),
        ),
        check_vma=False,
    )
```

profile of v0, /device:TPU:0, one launch (start us, length us, event | category | flops | bytes accessed | tf_op | source)
XLA Modules:
  0.0 719.6 jit_solution(13051128618466555613)
XLA Ops:
  8.4 1.3 fusion.32
  11.3 2.4 convolution_convert_fusion.7
  13.7 7.4 %all-to-all-start = ((bf16[16,20,3584]{2,1,0:T(8,128)(2,1)}), bf16[16,20,3584]{2,1,0:T(8,128)(2,1)S(1)}, u32[]{:S(2)}, u32[]{:S(2)}) async-start(bf16[16,20,3584]{2,1,0:T(8,128)(2,1)} %convolution_convert_fusion.7), calls=%async_computation | async-start | bytes 5505024 | tf_op jit(solution)/shard_map/all_to_all | solution.py:51
  21.1 52.5 %all-to-all-done = bf16[16,20,3584]{2,1,0:T(8,128)(2,1)S(1)} async-done(((bf16[16,20,3584]{2,1,0:T(8,128)(2,1)}), bf16[16,20,3584]{2,1,0:T(8,128)(2,1)S(1)}, u32[]{:S(2)}, u32[]{:S(2)}) %all-to-all-start) | async-done | bytes 2293792 | tf_op jit(solution)/shard_map/all_to_all | solution.py:51
  73.6 20.6 %conditional.4 = (bf16[320,3584]{1,0:T(8,128)(2,1)S(1)}) conditional(s32[]{:T(128)} %convert_element_type.159, () %tuple.32, (bf16[16,20,3584]{2,1,0:T(8,128)(2,1)S(1)}, bf16[3584,1024]{1,0:T(8,128)(2,1)}, bf16[3584,1024]{1,0:T(8,128)(2,1)}, bf16[1024,3584]{1,0:T(8,128)(2,1)}) %tuple.77), branch_computations={%region_4.5_spmd, %region_5.6_spmd} | conditional | flops 7049543680 | bytes 36110344 | solution.py:54
  73.6 2.1 reshape.292
  75.7 7.4 %fusion.113 = f32[320,1024]{1,0:T(8,128)} fusion(bf16[320,3584]{1,0:T(8,128)(2,1)} %reshape.292, bf16[3584,1024]{1,0:T(8,128)(2,1)} %get-tuple-element.49), kind=kOutput, calls=%fused_computation.201 | convolution fusion | flops 2348810240 | bytes 10944512 | tf_op jit(solution)/shard_map/cond/branch_1_fun/dot_general | solution.py:24
  83.1 11.2 %convolution_convert_fusion = bf16[320,3584]{1,0:T(8,128)(2,1)S(1)} fusion(bf16[1024,3584]{1,0:T(8,128)(2,1)} %get-tuple-element.51, bf16[320,3584]{1,0:T(8,128)(2,1)} %reshape.292, bf16[3584,1024]{1,0:T(8,128)(2,1)} %get-tuple-element.50, f32[320,1024]{1,0:T(8,128)} %fusion.113), kind=kOutput, calls=%fused_computation | convolution fusion | flops 4700733440 | bytes 20578304 | tf_op jit(solution)/shard_map/cond/branch_1_fun/dot_general | solution.py:27
  94.2 2.2 reshape.300
  96.5 14.0 %all-to-all-start.1 = ((bf16[16,20,3584]{2,1,0:T(8,128)(2,1)}), bf16[16,20,3584]{2,1,0:T(8,128)(2,1)S(1)}, u32[]{:S(2)}, u32[]{:S(2)}) async-start(bf16[16,20,3584]{2,1,0:T(8,128)(2,1)} %reshape.300), calls=%async_computation.1 | async-start | bytes 5505024 | tf_op jit(solution)/shard_map/all_to_all | solution.py:55
  110.5 52.4 %all-to-all-done.1 = bf16[16,20,3584]{2,1,0:T(8,128)(2,1)S(1)} async-done(((bf16[16,20,3584]{2,1,0:T(8,128)(2,1)}), bf16[16,20,3584]{2,1,0:T(8,128)(2,1)S(1)}, u32[]{:S(2)}, u32[]{:S(2)}) %all-to-all-start.1) | async-done | bytes 2293792 | tf_op jit(solution)/shard_map/all_to_all | solution.py:55
  163.0 2.1 fusion.12
  165.1 3.4 collective-permute-start
  168.5 1.3 collective-permute-start.1
  170.0 4.5 collective-permute-done
  174.5 4.0 collective-permute-done.1
  178.6 1.2 fusion.23
  180.6 2.4 convolution_convert_fusion.6
  183.0 13.4 %all-to-all-start.2 = ((bf16[16,20,3584]{2,1,0:T(8,128)(2,1)}), bf16[16,20,3584]{2,1,0:T(8,128)(2,1)S(1)}, u32[]{:S(2)}, u32[]{:S(2)}) async-start(bf16[16,20,3584]{2,1,0:T(8,128)(2,1)} %convolution_convert_fusion.6), calls=%async_computation.2 | async-start | bytes 5505024 | tf_op jit(solution)/shard_map/all_to_all | solution.py:51
  196.4 52.5 %all-to-all-done.2 = bf16[16,20,3584]{2,1,0:T(8,128)(2,1)S(1)} async-done(((bf16[16,20,3584]{2,1,0:T(8,128)(2,1)}), bf16[16,20,3584]{2,1,0:T(8,128)(2,1)S(1)}, u32[]{:S(2)}, u32[]{:S(2)}) %all-to-all-start.2) | async-done | bytes 2293792 | tf_op jit(solution)/shard_map/all_to_all | solution.py:51
  248.9 20.6 %conditional.5 = (bf16[320,3584]{1,0:T(8,128)(2,1)S(1)}) conditional(s32[]{:T(128)} %convert_element_type.167, () %tuple.34, (bf16[16,20,3584]{2,1,0:T(8,128)(2,1)S(1)}, bf16[3584,1024]{1,0:T(8,128)(2,1)}, bf16[3584,1024]{1,0:T(8,128)(2,1)}, bf16[1024,3584]{1,0:T(8,128)(2,1)}) %tuple.78), branch_computations={%region_10.11_spmd, %region_11.12_spmd} | conditional | flops 7049543680 | bytes 36110344 | solution.py:54
  248.9 2.1 reshape.293
  251.0 7.4 %fusion.114 = f32[320,1024]{1,0:T(8,128)} fusion(bf16[320,3584]{1,0:T(8,128)(2,1)} %reshape.293, bf16[3584,1024]{1,0:T(8,128)(2,1)} %get-tuple-element.53), kind=kOutput, calls=%fused_computation.202 | convolution fusion | flops 2348810240 | bytes 10944512 | tf_op jit(solution)/shard_map/cond/branch_1_fun/dot_general | solution.py:24
  258.4 11.2 %convolution_convert_fusion.1 = bf16[320,3584]{1,0:T(8,128)(2,1)S(1)} fusion(bf16[1024,3584]{1,0:T(8,128)(2,1)} %get-tuple-element.55, bf16[320,3584]{1,0:T(8,128)(2,1)} %reshape.293, bf16[3584,1024]{1,0:T(8,128)(2,1)} %get-tuple-element.54, f32[320,1024]{1,0:T(8,128)} %fusion.114), kind=kOutput, calls=%fused_computation.4 | convolution fusion | flops 4700733440 | bytes 20578304 | tf_op jit(solution)/shard_map/cond/branch_1_fun/dot_general | solution.py:27
  269.5 2.2 reshape.301
  271.8 13.8 %all-to-all-start.3 = ((bf16[16,20,3584]{2,1,0:T(8,128)(2,1)}), bf16[16,20,3584]{2,1,0:T(8,128)(2,1)S(1)}, u32[]{:S(2)}, u32[]{:S(2)}) async-start(bf16[16,20,3584]{2,1,0:T(8,128)(2,1)} %reshape.301), calls=%async_computation.3 | async-start | bytes 5505024 | tf_op jit(solution)/shard_map/all_to_all | solution.py:55
  285.6 52.5 %all-to-all-done.3 = bf16[16,20,3584]{2,1,0:T(8,128)(2,1)S(1)} async-done(((bf16[16,20,3584]{2,1,0:T(8,128)(2,1)}), bf16[16,20,3584]{2,1,0:T(8,128)(2,1)S(1)}, u32[]{:S(2)}, u32[]{:S(2)}) %all-to-all-start.3) | async-done | bytes 2293792 | tf_op jit(solution)/shard_map/all_to_all | solution.py:55
  338.1 2.1 fusion.13
  340.2 1.5 collective-permute-start.2
  341.8 1.3 collective-permute-start.3
  343.3 4.6 collective-permute-done.2
  347.9 4.0 collective-permute-done.3
  351.9 1.2 fusion.26
  353.9 2.4 convolution_convert_fusion.5
  356.4 13.4 %all-to-all-start.4 = ((bf16[16,20,3584]{2,1,0:T(8,128)(2,1)}), bf16[16,20,3584]{2,1,0:T(8,128)(2,1)S(1)}, u32[]{:S(2)}, u32[]{:S(2)}) async-start(bf16[16,20,3584]{2,1,0:T(8,128)(2,1)} %convolution_convert_fusion.5), calls=%async_computation.4 | async-start | bytes 5505024 | tf_op jit(solution)/shard_map/all_to_all | solution.py:51
  369.8 52.5 %all-to-all-done.4 = bf16[16,20,3584]{2,1,0:T(8,128)(2,1)S(1)} async-done(((bf16[16,20,3584]{2,1,0:T(8,128)(2,1)}), bf16[16,20,3584]{2,1,0:T(8,128)(2,1)S(1)}, u32[]{:S(2)}, u32[]{:S(2)}) %all-to-all-start.4) | async-done | bytes 2293792 | tf_op jit(solution)/shard_map/all_to_all | solution.py:51
  422.3 20.6 %conditional.6 = (bf16[320,3584]{1,0:T(8,128)(2,1)S(1)}) conditional(s32[]{:T(128)} %convert_element_type.175, () %tuple.36, (bf16[16,20,3584]{2,1,0:T(8,128)(2,1)S(1)}, bf16[3584,1024]{1,0:T(8,128)(2,1)}, bf16[3584,1024]{1,0:T(8,128)(2,1)}, bf16[1024,3584]{1,0:T(8,128)(2,1)}) %tuple.79), branch_computations={%region_16.17_spmd, %region_17.18_spmd} | conditional | flops 7049543680 | bytes 36110344 | solution.py:54
  422.3 2.1 reshape.294
  424.4 7.4 %fusion.115 = f32[320,1024]{1,0:T(8,128)} fusion(bf16[320,3584]{1,0:T(8,128)(2,1)} %reshape.294, bf16[3584,1024]{1,0:T(8,128)(2,1)} %get-tuple-element.57), kind=kOutput, calls=%fused_computation.203 | convolution fusion | flops 2348810240 | bytes 10944512 | tf_op jit(solution)/shard_map/cond/branch_1_fun/dot_general | solution.py:24
  431.7 11.2 %convolution_convert_fusion.2 = bf16[320,3584]{1,0:T(8,128)(2,1)S(1)} fusion(bf16[1024,3584]{1,0:T(8,128)(2,1)} %get-tuple-element.59, bf16[320,3584]{1,0:T(8,128)(2,1)} %reshape.294, bf16[3584,1024]{1,0:T(8,128)(2,1)} %get-tuple-element.58, f32[320,1024]{1,0:T(8,128)} %fusion.115), kind=kOutput, calls=%fused_computation.8 | convolution fusion | flops 4700733440 | bytes 20578304 | tf_op jit(solution)/shard_map/cond/branch_1_fun/dot_general | solution.py:27
  442.9 2.2 reshape.302
  445.1 13.8 %all-to-all-start.5 = ((bf16[16,20,3584]{2,1,0:T(8,128)(2,1)}), bf16[16,20,3584]{2,1,0:T(8,128)(2,1)S(1)}, u32[]{:S(2)}, u32[]{:S(2)}) async-start(bf16[16,20,3584]{2,1,0:T(8,128)(2,1)} %reshape.302), calls=%async_computation.5 | async-start | bytes 5505024 | tf_op jit(solution)/shard_map/all_to_all | solution.py:55
  459.0 52.5 %all-to-all-done.5 = bf16[16,20,3584]{2,1,0:T(8,128)(2,1)S(1)} async-done(((bf16[16,20,3584]{2,1,0:T(8,128)(2,1)}), bf16[16,20,3584]{2,1,0:T(8,128)(2,1)S(1)}, u32[]{:S(2)}, u32[]{:S(2)}) %all-to-all-start.5) | async-done | bytes 2293792 | tf_op jit(solution)/shard_map/all_to_all | solution.py:55
  511.5 2.1 fusion.14
  513.6 1.6 collective-permute-start.4
  515.2 1.3 collective-permute-start.5
  516.7 4.6 collective-permute-done.4
  521.3 4.0 collective-permute-done.5
  525.3 1.2 fusion.29
  527.3 2.4 convolution_convert_fusion.4
  529.7 13.4 %all-to-all-start.6 = ((bf16[16,20,3584]{2,1,0:T(8,128)(2,1)}), bf16[16,20,3584]{2,1,0:T(8,128)(2,1)S(1)}, u32[]{:S(2)}, u32[]{:S(2)}) async-start(bf16[16,20,3584]{2,1,0:T(8,128)(2,1)} %convolution_convert_fusion.4), calls=%async_computation.6 | async-start | bytes 5505024 | tf_op jit(solution)/shard_map/all_to_all | solution.py:51
  543.1 52.5 %all-to-all-done.6 = bf16[16,20,3584]{2,1,0:T(8,128)(2,1)S(1)} async-done(((bf16[16,20,3584]{2,1,0:T(8,128)(2,1)}), bf16[16,20,3584]{2,1,0:T(8,128)(2,1)S(1)}, u32[]{:S(2)}, u32[]{:S(2)}) %all-to-all-start.6) | async-done | bytes 2293792 | tf_op jit(solution)/shard_map/all_to_all | solution.py:51
  595.6 20.6 %conditional.7 = (bf16[320,3584]{1,0:T(8,128)(2,1)S(1)}) conditional(s32[]{:T(128)} %convert_element_type.183, () %tuple.38, (bf16[16,20,3584]{2,1,0:T(8,128)(2,1)S(1)}, bf16[3584,1024]{1,0:T(8,128)(2,1)}, bf16[3584,1024]{1,0:T(8,128)(2,1)}, bf16[1024,3584]{1,0:T(8,128)(2,1)}) %tuple.80), branch_computations={%region_22.23_spmd, %region_23.24_spmd} | conditional | flops 7049543680 | bytes 36110344 | solution.py:54
  595.6 2.1 reshape.295
  597.7 7.4 %fusion.116 = f32[320,1024]{1,0:T(8,128)} fusion(bf16[320,3584]{1,0:T(8,128)(2,1)} %reshape.295, bf16[3584,1024]{1,0:T(8,128)(2,1)} %get-tuple-element.61), kind=kOutput, calls=%fused_computation.204 | convolution fusion | flops 2348810240 | bytes 10944512 | tf_op jit(solution)/shard_map/cond/branch_1_fun/dot_general | solution.py:24
  605.1 11.2 %convolution_convert_fusion.3 = bf16[320,3584]{1,0:T(8,128)(2,1)S(1)} fusion(bf16[1024,3584]{1,0:T(8,128)(2,1)} %get-tuple-element.63, bf16[320,3584]{1,0:T(8,128)(2,1)} %reshape.295, bf16[3584,1024]{1,0:T(8,128)(2,1)} %get-tuple-element.62, f32[320,1024]{1,0:T(8,128)} %fusion.116), kind=kOutput, calls=%fused_computation.12 | convolution fusion | flops 4700733440 | bytes 20578304 | tf_op jit(solution)/shard_map/cond/branch_1_fun/dot_general | solution.py:27
  616.3 2.2 reshape.303
  618.5 14.0 %all-to-all-start.7 = ((bf16[16,20,3584]{2,1,0:T(8,128)(2,1)}), bf16[16,20,3584]{2,1,0:T(8,128)(2,1)S(1)}, u32[]{:S(2)}, u32[]{:S(2)}) async-start(bf16[16,20,3584]{2,1,0:T(8,128)(2,1)} %reshape.303), calls=%async_computation.7 | async-start | bytes 5505024 | tf_op jit(solution)/shard_map/all_to_all | solution.py:55
  632.6 2.2 convolution_convert_fusion.8
  634.8 2.3 copy.70
  637.2 70.3 %reduce-scatter.4.cloned.1.call-done = bf16[224,64]{1,0:T(8,128)(2,1)} async-done(((bf16[3584,64]{1,0:T(8,128)(2,1)}), bf16[224,64]{1,0:T(8,128)(2,1)}) %reduce-scatter.4.cloned.1.call-update) | async-done | bytes 28688
  707.5 0.9 copy.71
  709.0 1.4 fusion.15
  710.5 2.3 select_select_fusion
  (64 shorter events, 6.7 us)
Async XLA Ops:
  10.6 0.7 copy-start.1
  13.7 59.9 %all-to-all-start = ((bf16[16,20,3584]{2,1,0:T(8,128)(2,1)}), bf16[16,20,3584]{2,1,0:T(8,128)(2,1)S(1)}, u32[]{:S(2)}, u32[]{:S(2)}) async-start(bf16[16,20,3584]{2,1,0:T(8,128)(2,1)} %convolution_convert_fusion.7), calls=%async_computation | async-start | bytes 5505024 | tf_op jit(solution)/shard_map/all_to_all | solution.py:51
  96.4 14.0 %copy-start.8 = (f32[1,2,32,8]{2,3,1,0:T(8,128)S(1)}, f32[1,2,32,8]{2,3,1,0:T(8,128)}, u32[]{:S(2)}) copy-start(f32[1,2,32,8]{2,3,1,0:T(8,128)} %param.26) | copy-start | bytes 6148
  96.5 14.0 %copy-start.9 = (f32[1,2,32,8]{2,3,1,0:T(8,128)S(1)}, f32[1,2,32,8]{2,3,1,0:T(8,128)}, u32[]{:S(2)}) copy-start(f32[1,2,32,8]{2,3,1,0:T(8,128)} %param.28) | copy-start | bytes 6148
  96.5 66.5 %all-to-all-start.1 = ((bf16[16,20,3584]{2,1,0:T(8,128)(2,1)}), bf16[16,20,3584]{2,1,0:T(8,128)(2,1)S(1)}, u32[]{:S(2)}, u32[]{:S(2)}) async-start(bf16[16,20,3584]{2,1,0:T(8,128)(2,1)} %reshape.300), calls=%async_computation.1 | async-start | bytes 5505024 | tf_op jit(solution)/shard_map/all_to_all | solution.py:55
  110.5 68.1 %copy-start = (bf16[2,32,3584]{2,1,0:T(8,128)(2,1)S(1)}, bf16[2,32,3584]{2,1,0:T(8,128)(2,1)}, u32[]{:S(2)}) copy-start(bf16[2,32,3584]{2,1,0:T(8,128)(2,1)} %param.20) | copy-start | bytes 1376260
  165.1 9.4 %collective-permute-start = (bf16[32,3584]{1,0:T(8,128)(2,1)}, bf16[32,3584]{1,0:T(8,128)(2,1)S(1)}, u32[]{:S(2)}, u32[]{:S(2)}) collective-permute-start(bf16[32,3584]{1,0:T(8,128)(2,1)} %fusion.12), channel_id=1, source_target_pairs={{0,16},{1,17},{2,18},{3,19},{4,20},{5,21},{6,22},{7,23},{8,24},{9,... | collective-permute-start | bytes 688136 | tf_op jit(solution)/shard_map/ppermute | solution.py:14
  168.5 10.1 %collective-permute-start.1 = (bf16[32,3584]{1,0:T(8,128)(2,1)}, bf16[32,3584]{1,0:T(8,128)(2,1)S(1)}, u32[]{:S(2)}, u32[]{:S(2)}) collective-permute-start(bf16[32,3584]{1,0:T(8,128)(2,1)} %fusion.12), channel_id=1, source_target_pairs={{16,0},{17,1},{18,2},{19,3},{20,4},{21,5},{22,6},{23,7},{24,8},{25... | collective-permute-start | bytes 688136 | tf_op jit(solution)/shard_map/ppermute | solution.py:14
  179.9 0.7 copy-start.3
  183.0 65.9 %all-to-all-start.2 = ((bf16[16,20,3584]{2,1,0:T(8,128)(2,1)}), bf16[16,20,3584]{2,1,0:T(8,128)(2,1)S(1)}, u32[]{:S(2)}, u32[]{:S(2)}) async-start(bf16[16,20,3584]{2,1,0:T(8,128)(2,1)} %convolution_convert_fusion.6), calls=%async_computation.2 | async-start | bytes 5505024 | tf_op jit(solution)/shard_map/all_to_all | solution.py:51
  271.8 66.4 %all-to-all-start.3 = ((bf16[16,20,3584]{2,1,0:T(8,128)(2,1)}), bf16[16,20,3584]{2,1,0:T(8,128)(2,1)S(1)}, u32[]{:S(2)}, u32[]{:S(2)}) async-start(bf16[16,20,3584]{2,1,0:T(8,128)(2,1)} %reshape.301), calls=%async_computation.3 | async-start | bytes 5505024 | tf_op jit(solution)/shard_map/all_to_all | solution.py:55
  340.2 7.7 %collective-permute-start.2 = (bf16[32,3584]{1,0:T(8,128)(2,1)}, bf16[32,3584]{1,0:T(8,128)(2,1)S(1)}, u32[]{:S(2)}, u32[]{:S(2)}) collective-permute-start(bf16[32,3584]{1,0:T(8,128)(2,1)} %fusion.13), channel_id=1, source_target_pairs={{0,16},{1,17},{2,18},{3,19},{4,20},{5,21},{6,22},{7,23},{8,24},{9,... | collective-permute-start | bytes 688136 | tf_op jit(solution)/shard_map/ppermute | solution.py:14
  341.8 10.1 %collective-permute-start.3 = (bf16[32,3584]{1,0:T(8,128)(2,1)}, bf16[32,3584]{1,0:T(8,128)(2,1)S(1)}, u32[]{:S(2)}, u32[]{:S(2)}) collective-permute-start(bf16[32,3584]{1,0:T(8,128)(2,1)} %fusion.13), channel_id=1, source_target_pairs={{16,0},{17,1},{18,2},{19,3},{20,4},{21,5},{22,6},{23,7},{24,8},{25... | collective-permute-start | bytes 688136 | tf_op jit(solution)/shard_map/ppermute | solution.py:14
  353.3 0.7 copy-start.5
  356.4 65.9 %all-to-all-start.4 = ((bf16[16,20,3584]{2,1,0:T(8,128)(2,1)}), bf16[16,20,3584]{2,1,0:T(8,128)(2,1)S(1)}, u32[]{:S(2)}, u32[]{:S(2)}) async-start(bf16[16,20,3584]{2,1,0:T(8,128)(2,1)} %convolution_convert_fusion.5), calls=%async_computation.4 | async-start | bytes 5505024 | tf_op jit(solution)/shard_map/all_to_all | solution.py:51
  445.1 66.4 %all-to-all-start.5 = ((bf16[16,20,3584]{2,1,0:T(8,128)(2,1)}), bf16[16,20,3584]{2,1,0:T(8,128)(2,1)S(1)}, u32[]{:S(2)}, u32[]{:S(2)}) async-start(bf16[16,20,3584]{2,1,0:T(8,128)(2,1)} %reshape.302), calls=%async_computation.5 | async-start | bytes 5505024 | tf_op jit(solution)/shard_map/all_to_all | solution.py:55
  513.6 7.7 %collective-permute-start.4 = (bf16[32,3584]{1,0:T(8,128)(2,1)}, bf16[32,3584]{1,0:T(8,128)(2,1)S(1)}, u32[]{:S(2)}, u32[]{:S(2)}) collective-permute-start(bf16[32,3584]{1,0:T(8,128)(2,1)} %fusion.14), channel_id=1, source_target_pairs={{0,16},{1,17},{2,18},{3,19},{4,20},{5,21},{6,22},{7,23},{8,24},{9,... | collective-permute-start | bytes 688136 | tf_op jit(solution)/shard_map/ppermute | solution.py:14
  515.2 10.1 %collective-permute-start.5 = (bf16[32,3584]{1,0:T(8,128)(2,1)}, bf16[32,3584]{1,0:T(8,128)(2,1)S(1)}, u32[]{:S(2)}, u32[]{:S(2)}) collective-permute-start(bf16[32,3584]{1,0:T(8,128)(2,1)} %fusion.14), channel_id=1, source_target_pairs={{16,0},{17,1},{18,2},{19,3},{20,4},{21,5},{22,6},{23,7},{24,8},{25... | collective-permute-start | bytes 688136 | tf_op jit(solution)/shard_map/ppermute | solution.py:14
  526.6 0.7 copy-start.6
  529.7 65.9 %all-to-all-start.6 = ((bf16[16,20,3584]{2,1,0:T(8,128)(2,1)}), bf16[16,20,3584]{2,1,0:T(8,128)(2,1)S(1)}, u32[]{:S(2)}, u32[]{:S(2)}) async-start(bf16[16,20,3584]{2,1,0:T(8,128)(2,1)} %convolution_convert_fusion.4), calls=%async_computation.6 | async-start | bytes 5505024 | tf_op jit(solution)/shard_map/all_to_all | solution.py:51
  618.5 14.1 %copy-start.7 = (bf16[1,2,2,32,64]{4,3,2,1,0:T(8,128)(2,1)S(1)}, bf16[1,2,2,32,64]{4,3,2,1,0:T(8,128)(2,1)}, u32[]{:S(2)}) copy-start(bf16[1,2,2,32,64]{4,3,2,1,0:T(8,128)(2,1)} %param.29) | copy-start | bytes 49156
  618.5 14.1 %copy-start.2 = (bf16[32,3584]{1,0:T(8,128)(2,1)S(1)}, bf16[32,3584]{1,0:T(8,128)(2,1)}, u32[]{:S(2)}) copy-start(bf16[32,3584]{1,0:T(8,128)(2,1)} %copy-done.1) | copy-start | bytes 688132
  618.5 14.1 %copy-start.4 = (bf16[32,3584]{1,0:T(8,128)(2,1)S(1)}, bf16[32,3584]{1,0:T(8,128)(2,1)}, u32[]{:S(2)}) copy-start(bf16[32,3584]{1,0:T(8,128)(2,1)} %copy-done.3) | copy-start | bytes 688132
  618.5 90.5 %all-to-all-start.7 = ((bf16[16,20,3584]{2,1,0:T(8,128)(2,1)}), bf16[16,20,3584]{2,1,0:T(8,128)(2,1)S(1)}, u32[]{:S(2)}, u32[]{:S(2)}) async-start(bf16[16,20,3584]{2,1,0:T(8,128)(2,1)} %reshape.303), calls=%async_computation.7 | async-start | bytes 5505024 | tf_op jit(solution)/shard_map/all_to_all | solution.py:55
  632.5 75.0 %reduce-scatter.4.cloned.1.call-start = ((), (), s32[]{:S(2)}) async-start(), calls=%async_computation.9 | async-start | bytes 974848
Sparse Core Ops, SparseCore 0:
  637.2 70.2 reduce-scatter.3
where the time goes:
time: 721 us; the launch traced here: 720 us
  waiting for transfers between devices  463 us (64%)
  starting transfers between devices  114 us (16%)
  matrix products  93.8 us (13%)
  local copies, waits for them, and re-layouts  23.7 us (3%)
  between operations  14.7 us (2%)
  other arithmetic  10.4 us (1%)
    all_to_all x4, waiting for transfers between devices, run_layer(): lax.all_to_all(outgoing, 'expert', split_axis=0, concat_axis=0, tiled=True)  210 us
    all_to_all x4, waiting for transfers between devices, run_layer(): lax.all_to_all(finished.reshape(source_count, item_count, feature_count),...  157 us
    unnamed x2, waiting for transfers between devices  70.3 us
    all_to_all x4, starting transfers between devices, run_layer(): lax.all_to_all(finished.reshape(source_count, item_count, feature_count),...  55.6 us
    all_to_all x4, starting transfers between devices, run_layer(): lax.all_to_all(outgoing, 'expert', split_axis=0, concat_axis=0, tiled=True)  47.5 us
    dot_general x4, matrix products, expert_rows(): jnp.dot(hidden, down_mat, preferred_element_type=jnp.float32)  44.6 us
    dot_general x4, matrix products, expert_rows(): gate_act = jnp.dot(row_block, gate_mat, preferred_element_type=jnp.float32)  29.5 us
    ppermute x6, waiting for transfers between devices, passed_along(): lax.ppermute(value, axis, [(source, source + steps) for source in range(f...  25.8 us
  transfers between devices with their start and end apart: 15, of which 14 were waited for; matrix products, arithmetic and copies ran while one was open for 1% of the time, Pallas kernels for 0%

commit v1 on v0

v1 whole, which is shorter than its diff:
```python
from functools import partial

import jax
import jax.numpy as jnp
from jax import lax
from jax.experimental import pallas as pl
from jax.experimental.pallas import tpu as pltpu
from jax.sharding import PartitionSpec as P

EPSILON = 1e-06
LANES = 128
MESH = pl.DeviceIdType.MESH


def grid_of(count):
    chips = count // 2
    bits = chips.bit_length() - 1
    far = 1 << ((bits + 1) // 2)
    return far, chips // far


def flipped(value, mask):
    result, bit = value, 1
    while bit <= mask:
        if mask & bit:
            result = result + bit - 2 * bit * ((value // bit) % 2)
        bit *= 2
    return result


def layer_kernel(
    count, far, near, window,
    x_ref, carried_ref, gate_hbm, up_hbm, down_hbm,
    out_ref, kr_ref,
    rows, w_gate, w_up, w_down, hidden, core_in, near_in, far_in,
    w_sem, z_send, y_send, c_send, ag_recv,
    rc_send, rc_recv, ry_send, ry_recv, rz_send, rz_recv,
):
    micro, tokens, width = x_ref.shape
    features, units = w_gate.shape
    lane_rows = near * far * tokens
    me = lax.axis_index("expert")
    pipe = lax.axis_index("pipe")
    c = me % 2
    y = (me // 2) % near
    z = me // (2 * near)

    def device(cc, yy, zz):
        return (pipe, (zz * near + yy) * 2 + cc)

    def slot(cc, yy, zz):
        return (cc * near + yy) * far + zz

    def span(cc, yy, zz):
        return pl.ds(pl.multiple_of(slot(cc, yy, zz) * tokens, tokens), tokens)

    def lane_span(cc):
        return pl.ds(pl.multiple_of(cc * lane_rows, lane_rows), lane_rows)

    core_peer = device(1 - c, y, z)
    near_peers = {k: device(c, flipped(y, k), z) for k in range(1, near)}
    far_peers = {k: device(c, y, flipped(z, k)) for k in range(1, far)}
    partners = [core_peer] + list(near_peers.values()) + list(far_peers.values())

    loads = [
        pltpu.make_async_copy(gate_hbm, w_gate, w_sem.at[0]),
        pltpu.make_async_copy(up_hbm, w_up, w_sem.at[1]),
        pltpu.make_async_copy(down_hbm, w_down, w_sem.at[2]),
    ]
    for load in loads:
        load.start()

    barrier = pltpu.get_barrier_semaphore()
    for partner in partners:
        pl.semaphore_signal(barrier, inc=1, device_id=partner, device_id_type=MESH)
    pl.semaphore_wait(barrier, len(partners))

    kr_ref[...] = jnp.zeros_like(kr_ref)
    window_start = jnp.minimum(me * (features // count) // LANES * LANES, width - window)

    def move(m, cc, yy, zz, send_sem, target):
        where = rows.at[m, span(cc, yy, zz)]
        return pltpu.make_async_remote_copy(
            src_ref=where, dst_ref=where, send_sem=send_sem,
            recv_sem=ag_recv.at[m, slot(cc, yy, zz)], device_id=target, device_id_type=MESH,
        )

    def arrived(m, cc, yy, zz):
        move(m, cc, yy, zz, z_send.at[m, 0], core_peer).wait_recv()

    sends = [[] for _ in range(micro)]

    def start(m, copy):
        copy.start()
        sends[m].append(copy)

    def to_near(m, k):
        zz = flipped(z, k)
        for j in range(1, near):
            start(m, move(m, c, y, zz, y_send.at[m, j * far + k], near_peers[j]))

    def to_core(m, j, k):
        start(m, move(m, c, flipped(y, j), flipped(z, k), c_send.at[m, j * far + k], core_peer))

    def gather_start(m):
        rows[m, span(c, y, z)] = x_ref[m]
        for k in range(1, far):
            start(m, move(m, c, y, z, z_send.at[m, k], far_peers[k]))
        to_near(m, 0)
        to_core(m, 0, 0)

    def gather_far(m):
        for k in range(1, far):
            arrived(m, c, y, flipped(z, k))
            to_near(m, k)
            to_core(m, 0, k)

    def gather_near(m):
        for k in range(far):
            for j in range(1, near):
                arrived(m, c, flipped(y, j), flipped(z, k))
                to_core(m, j, k)

    def gather_core(m):
        for k in range(far):
            for j in range(near):
                arrived(m, 1 - c, flipped(y, j), flipped(z, k))
        for copy in sends[m]:
            copy.wait_send()

    unit_tile = 256 if units % 256 == 0 else units
    feature_tile = 512 if features % 512 == 0 else features

    def expand(m, cc):
        here = lane_span(cc)
        kr_ref[...] += lax.dot_general(
            rows[m, here, pl.ds(features, width - features)],
            rows[m, here, pl.ds(pl.multiple_of(window_start, LANES), window)],
            (((0,), (0,)), ((), ())), preferred_element_type=jnp.float32,
        )

        def body(i, carry):
            tile = pl.ds(pl.multiple_of(i * unit_tile, unit_tile), unit_tile)
            block = rows[m, here, pl.ds(0, features)]
            gate = jnp.dot(block, w_gate[:, tile], preferred_element_type=jnp.float32)
            up = jnp.dot(block, w_up[:, tile], preferred_element_type=jnp.float32)
            hidden[:, tile] = (gate / (1.0 + jnp.exp(-gate)) * up).astype(jnp.bfloat16)
            return carry

        lax.fori_loop(0, units // unit_tile, body, 0)

    def contract(m, cc, add):
        here = lane_span(cc)
        extra = rows[m, here, pl.ds(features, width - features)].astype(jnp.float32)
        lane = lax.broadcasted_iota(jnp.int32, extra.shape, 1)
        mine = (lane == me) | (lane == count + me)
        weight = jnp.sum(jnp.where(mine, extra, 0.0), axis=1, keepdims=True)

        def body(i, carry):
            tile = pl.ds(pl.multiple_of(i * feature_tile, feature_tile), feature_tile)
            part = jnp.dot(hidden[...], w_down[:, tile], preferred_element_type=jnp.float32) * weight
            if add:
                part = part + core_in[m, :, tile].astype(jnp.float32)
            rows[m, here, tile] = part.astype(jnp.bfloat16)
            return carry

        lax.fori_loop(0, features // feature_tile, body, 0)

    columns = pl.ds(0, features)

    def core_sum(m):
        return pltpu.make_async_remote_copy(
            src_ref=rows.at[m, lane_span(1 - c), columns], dst_ref=core_in.at[m],
            send_sem=rc_send.at[m], recv_sem=rc_recv.at[m],
            device_id=core_peer, device_id_type=MESH,
        )

    def near_sum(m, j, k):
        zz = flipped(z, k)
        return pltpu.make_async_remote_copy(
            src_ref=rows.at[m, span(c, flipped(y, j), zz), columns],
            dst_ref=near_in.at[m, j - 1, zz],
            send_sem=ry_send.at[m, j - 1, zz], recv_sem=ry_recv.at[m, j - 1, zz],
            device_id=near_peers[j], device_id_type=MESH,
        )

    def far_sum(m, k):
        return pltpu.make_async_remote_copy(
            src_ref=rows.at[m, span(c, y, flipped(z, k)), columns],
            dst_ref=far_in.at[m, k - 1],
            send_sem=rz_send.at[m, k - 1], recv_sem=rz_recv.at[m, k - 1],
            device_id=far_peers[k], device_id_type=MESH,
        )

    far_order = list(range(far - 1, -1, -1))

    def near_start(m):
        for k in far_order:
            for j in range(1, near):
                near_sum(m, j, k).start()

    def near_finish(m):
        for k in far_order:
            here = span(c, y, flipped(z, k))
            total = rows[m, here, columns].astype(jnp.float32)
            for j in range(1, near):
                near_sum(m, j, k).wait_recv()
                total = total + near_in[m, j - 1, flipped(z, k)].astype(jnp.float32)
            rows[m, here, columns] = total.astype(jnp.bfloat16)
            if k > 0:
                far_sum(m, k).start()

    def far_finish(m):
        total = carried_ref[m].astype(jnp.float32) + rows[m, span(c, y, z), columns].astype(jnp.float32)
        for k in range(1, far):
            far_sum(m, k).wait_recv()
            total = total + far_in[m, k - 1].astype(jnp.float32)
        out_ref[m] = total.astype(jnp.bfloat16)

    gather_start(0)
    gather_far(0)
    for m in range(micro):
        later, before = m + 1 < micro, m > 0
        if later:
            gather_start(m + 1)
        if m == 0:
            gather_near(0)
        gather_core(m)
        if m == 0:
            loads[0].wait()
            loads[1].wait()
        expand(m, 1 - c)
        if later:
            gather_far(m + 1)
        if before:
            near_finish(m - 1)
        if m == 0:
            loads[2].wait()
        contract(m, 1 - c, False)
        core_sum(m).start()
        expand(m, c)
        if later:
            gather_near(m + 1)
        if before:
            far_finish(m - 1)
        core_sum(m).wait_recv()
        contract(m, c, True)
        near_start(m)
    near_finish(micro - 1)
    far_finish(micro - 1)
    for m in range(micro):
        core_sum(m).wait_send()
        for k in range(far):
            for j in range(1, near):
                near_sum(m, j, k).wait_send()
            if k > 0:
                far_sum(m, k).wait_send()


def run_layer(x, carried, w_gate, w_up, w_down, count):
    far, near = grid_of(count)
    micro, tokens, width = x.shape
    features, units = w_gate.shape
    lane_rows = near * far * tokens
    share = features // count
    window = -(-(share + LANES - 1) // LANES) * LANES
    bf16 = jnp.bfloat16
    dma = pltpu.SemaphoreType.DMA
    total_rows = 2 * lane_rows * micro
    return pl.pallas_call(
        partial(layer_kernel, count, far, near, window),
        out_shape=(
            jax.ShapeDtypeStruct(carried.shape, bf16),
            jax.ShapeDtypeStruct((width - features, window), jnp.float32),
        ),
        in_specs=[pl.BlockSpec(memory_space=pltpu.VMEM)] * 2 + [pl.BlockSpec(memory_space=pl.ANY)] * 3,
        out_specs=(pl.BlockSpec(memory_space=pltpu.VMEM),) * 2,
        scratch_shapes=[
            pltpu.VMEM((micro, 2 * lane_rows, width), bf16),
            pltpu.VMEM(w_gate.shape, bf16),
            pltpu.VMEM(w_up.shape, bf16),
            pltpu.VMEM(w_down.shape, bf16),
            pltpu.VMEM((lane_rows, units), bf16),
            pltpu.VMEM((micro, lane_rows, features), bf16),
            pltpu.VMEM((micro, near - 1, far, tokens, features), bf16),
            pltpu.VMEM((micro, far - 1, tokens, features), bf16),
            dma((3,)),
            dma((micro, far)),
            dma((micro, near * far)),
            dma((micro, near * far)),
            dma((micro, count)),
            dma((micro,)),
            dma((micro,)),
            dma((micro, near - 1, far)),
            dma((micro, near - 1, far)),
            dma((micro, far - 1)),
            dma((micro, far - 1)),
        ],
        compiler_params=pltpu.CompilerParams(
            collective_id=0, has_side_effects=True, vmem_limit_bytes=60 * 1024 * 1024
        ),
        cost_estimate=pl.CostEstimate(
            flops=6 * total_rows * features * units,
            bytes_accessed=6 * features * units,
            transcendentals=total_rows * units,
        ),
    )(x, carried, w_gate, w_up, w_down)


def normalize(carried, norm_scale):
    values = carried.astype(jnp.float32)
    inv_rms = lax.rsqrt(jnp.mean(values * values, axis=-1, keepdims=True) + EPSILON)
    return (values * inv_rms * norm_scale).astype(jnp.bfloat16)


def side_columns(ids, gates, tangents, count, width):
    named = (ids[..., None] == jnp.arange(count, dtype=jnp.int32)).astype(jnp.float32)
    weight = jnp.sum(gates[..., None] * named, axis=-2)
    high = weight.astype(jnp.bfloat16)
    low = (weight - high.astype(jnp.float32)).astype(jnp.bfloat16)
    side = jnp.concatenate([high, low, tangents], axis=-1)
    return jnp.pad(side, ((0, 0), (0, 0), (0, width - side.shape[-1])))


def on_device(
    down_tokens,
    up_tokens,
    norm_gain,
    w_gate,
    w_up,
    w_down,
    down_ids,
    down_gates,
    up_ids,
    up_gates,
    key_cotangent,
):
    sections = lax.axis_size("pipe")
    section = lax.axis_index("pipe")
    count = lax.axis_size("expert")
    features = down_tokens.shape[-1]
    rope = key_cotangent.shape[-1]
    share = features // count
    side_width = -(-(2 * count + rope) // LANES) * LANES
    window = -(-(share + LANES - 1) // LANES) * LANES
    side_down = side_columns(down_ids[0], down_gates[0], key_cotangent[0, 0], count, side_width)
    side_up = side_columns(up_ids[0], up_gates[0], key_cotangent[0, 1], count, side_width)
    carried = jnp.where(section == 0, down_tokens, up_tokens)
    down_states = jnp.zeros_like(down_tokens)
    up_states = jnp.zeros_like(up_tokens)
    key_grad = 0.0
    for turn in range(sections):
        down_on = section == turn
        up_on = section == sections - 1 - turn
        side = jnp.where(down_on, side_down, side_up)
        side = jnp.where(down_on | up_on, side, jnp.zeros_like(side))
        x = jnp.concatenate([normalize(carried, norm_gain[0]), side], axis=-1)
        output, grad = run_layer(x, carried, w_gate[0, 0], w_up[0, 0], w_down[0, 0], count)
        key_grad = key_grad + grad
        down_states = jnp.where(down_on, output, down_states)
        up_states = jnp.where(up_on, output, up_states)
        if turn + 1 < sections:
            carried = lax.ppermute(
                output, "pipe", [(turn, turn + 1), (sections - 1 - turn, sections - 2 - turn)]
            )
    first = lax.axis_index("expert") * share
    start = jnp.minimum(first // LANES * LANES, features + side_width - window)
    grad_rows = lax.dynamic_slice(key_grad, (2 * count, first - start), (rope, share)).T
    return (down_states[None], up_states[None], grad_rows[None])


def solution(mesh):
    return jax.shard_map(
        on_device,
        mesh=mesh,
        in_specs=(
            P(None, "expert", None),
            P(None, "expert", None),
            P("pipe", None),
            P("pipe", "expert", None, None),
            P("pipe", "expert", None, None),
            P("pipe", "expert", None, None),
            P("pipe", None, "expert", None),
            P("pipe", None, "expert", None),
            P("pipe", None, "expert", None),
            P("pipe", None, "expert", None),
            P("pipe", None, None, "expert", None),
        ),
        out_specs=(
            P("pipe", None, "expert", None),
            P("pipe", None, "expert", None),
            P("pipe", "expert", None),
        ),
        check_vma=False,
    )
```

time: 721 us -> 266 us (0.37)
  waiting for transfers between devices: 463 us -> 7.25 us
  Pallas kernels: 0 us -> 245 us
  starting transfers between devices: 114 us -> 1.56 us
  matrix products: 93.8 us -> 0 us
  local copies, waits for them, and re-layouts: 23.7 us -> 1.09 us
  between operations: 14.7 us -> 0.72 us
    all_to_all x8 -> x0, waiting for transfers between devices: 367 us -> none  [the longest x4 210 us: run_layer(): lax.all_to_all(outgoing, 'expert', split_axis=0, concat_axis=0, tiled=True)]
    pallas_call x0 -> x2, Pallas kernels: none -> 245 us  [run_layer(): pl.pallas_call(partial(layer_kernel, count, far, near, window), out_shape...]
    all_to_all x8 -> x0, starting transfers between devices: 103 us -> none  [the longest x4 55.6 us: run_layer(): lax.all_to_all(finished.reshape(source_count, item_count, feature_count),...]
    dot_general x17 -> x0, matrix products: 93.8 us -> none  [the longest x4 44.6 us: expert_rows(): jnp.dot(hidden, down_mat, preferred_element_type=jnp.float32)]
    unnamed x2 -> x0, waiting for transfers between devices: 70.3 us -> none
    ppermute x6 -> x1, waiting for transfers between devices: 25.8 us -> 7.25 us  [on_device(): lax.ppermute(output, 'pipe', [(turn, turn + 1), (sections - 1 - turn, sec...]
    reshape x8 -> x0, local copies, waits for them, and re-layouts: 17.2 us -> none  [the longest x4 8.84 us: run_layer(): finished.reshape(source_count, item_count, feature_count)]
    ppermute x6 -> x1, starting transfers between devices: 10.3 us -> 1.56 us  [on_device(): lax.ppermute(output, 'pipe', [(turn, turn + 1), (sections - 1 - turn, sec...]
  transfers between devices with their start and end apart: 15 -> 1, of which waited for: 14 -> 1; matrix products, arithmetic and copies ran while one was open for 1% -> 0% of each run, Pallas kernels for 0% -> 0%
where the time goes in v1:
time: 266 us; the launch traced here: 265 us
  Pallas kernels  245 us (92%)
  other arithmetic  9.48 us (4%)
  waiting for transfers between devices  7.25 us (3%)
    pallas_call x2, Pallas kernels, run_layer(): pl.pallas_call(partial(layer_kernel, count, far, near, window), out_shape...  245 us
    ppermute x1, waiting for transfers between devices, on_device(): lax.ppermute(output, 'pipe', [(turn, turn + 1), (sections - 1 - turn, sec...  7.25 us
  transfers between devices with their start and end apart: 1, of which 1 were waited for; matrix products, arithmetic and copies ran while one was open for 0% of the time, Pallas kernels for 0%

profile of v1, /device:TPU:0, one launch (start us, length us, event | category | flops | bytes accessed | tf_op | source)
XLA Modules:
  0.0 265.5 jit_solution(14216938538241321157)
XLA Ops:
  0.6 0.7 select_reduce_fusion
  1.4 0.1 copy.26
  1.5 0.7 select_reduce_fusion.1
  2.2 0.1 copy.23
  2.3 0.1 copy.24
  2.4 0.1 copy.27
  2.5 0.7 slice_bitcast_fusion.1
  3.2 1.3 fusion
  4.5 0.0 copy-start.1
  4.5 0.8 reduce
  5.3 0.2 fusion.2
  5.5 0.1 select_select_fusion.1
  5.6 0.8 pad_maximum_fusion.x_ref
  6.4 0.0 copy-done.1
  6.4 122.7 %shard_map.130 = (bf16[2,32,3584]{2,1,0:T(8,128)(2,1)}, f32[128,384]{1,0:T(8,128)}) custom-call(bf16[2,32,3712]{2,1,0:T(8,128)(2,1)} %pad_maximum_fusion.x_ref, bf16[2,32,3584]{2,1,0:T(8,128)(2,1)} %copy-done.1, bf16[3584,1024]{1,0:T(8,128)(2,1)} %bitcast.23, bf16[3584,1024]{1,0:T(8,128)(2,1)} %bitcast.25, bf16[1024,3584]{1,0:T(8,128)(2,1)} %bitcast.27), custom_call_target="tpu_custom_call" | custom-call | flops 22548578304 | bytes 22020096 | tf_op jit(solution)/shard_map/pallas_call | solution.py:270
  129.1 1.6 collective-permute-start
  130.6 7.2 %collective-permute-done.carried_ref = bf16[2,32,3584]{2,1,0:T(8,128)(2,1)S(1)} collective-permute-done((bf16[2,32,3584]{2,1,0:T(8,128)(2,1)}, bf16[2,32,3584]{2,1,0:T(8,128)(2,1)S(1)}, u32[]{:S(2)}, u32[]{:S(2)}) %collective-permute-start) | collective-permute-done | bytes 458784 | tf_op jit(solution)/shard_map/ppermute | solution.py:363
  137.9 0.0 copy-start
  137.9 0.2 fusion.3
  138.1 0.2 fusion.5
  138.3 0.8 pad_maximum_fusion.1.x_ref
  139.1 0.0 copy-done
  139.1 0.0 copy-start.2
  139.1 122.7 %shard_map.131 = (bf16[2,32,3584]{2,1,0:T(8,128)(2,1)}, f32[128,384]{1,0:T(8,128)}) custom-call(bf16[2,32,3712]{2,1,0:T(8,128)(2,1)} %pad_maximum_fusion.1.x_ref, bf16[2,32,3584]{2,1,0:T(8,128)(2,1)} %copy-done, bf16[3584,1024]{1,0:T(8,128)(2,1)} %bitcast.24, bf16[3584,1024]{1,0:T(8,128)(2,1)} %bitcast.26, bf16[1024,3584]{1,0:T(8,128)(2,1)} %bitcast.28), custom_call_target="tpu_custom_call" | custom-call | flops 22548578304 | bytes 22020096 | tf_op jit(solution)/shard_map/pallas_call | solution.py:270
  261.8 0.0 copy-done.2
  261.8 2.0 select_bitcast_fusion
  263.8 1.7 fusion.6
  (5 shorter events, 0.0 us)
Async XLA Ops:
  4.5 1.9 copy-start.1
  129.1 8.8 %collective-permute-start = (bf16[2,32,3584]{2,1,0:T(8,128)(2,1)}, bf16[2,32,3584]{2,1,0:T(8,128)(2,1)S(1)}, u32[]{:S(2)}, u32[]{:S(2)}) collective-permute-start(bf16[2,32,3584]{2,1,0:T(8,128)(2,1)} %get-tuple-element.7), channel_id=1, source_target_pairs={{0,16},{16,0},{1,17},{17,1},{2,18},{18,2},{3,19},{19,3},{4,20},{20... | collective-permute-start | bytes 1376264 | tf_op jit(solution)/shard_map/ppermute | solution.py:363
  137.9 1.2 copy-start
  139.1 122.7 %copy-start.2 = (bf16[2,32,3584]{2,1,0:T(8,128)(2,1)S(1)}, bf16[2,32,3584]{2,1,0:T(8,128)(2,1)}, u32[]{:S(2)}) copy-start(bf16[2,32,3584]{2,1,0:T(8,128)(2,1)} %get-tuple-element.7) | copy-start | bytes 1376260

commit v2 on v1

--- a/solution.py
+++ b/solution.py
@@ -88,56 +88,77 @@
     def arrived(m, cc, yy, zz):
         move(m, cc, yy, zz, z_send.at[m, 0], core_peer).wait_recv()
 
-    sends = [[] for _ in range(micro)]
-
-    def start(m, copy):
-        copy.start()
-        sends[m].append(copy)
-
-    def to_near(m, k):
-        zz = flipped(z, k)
-        for j in range(1, near):
-            start(m, move(m, c, y, zz, y_send.at[m, j * far + k], near_peers[j]))
-
-    def to_core(m, j, k):
-        start(m, move(m, c, flipped(y, j), flipped(z, k), c_send.at[m, j * far + k], core_peer))
+    def to_near(m, zz):
+        return [move(m, c, y, zz, y_send.at[m, j * far + zz], near_peers[j]) for j in range(1, near)]
+
+    def to_core(m, j, zz):
+        return move(m, c, flipped(y, j), zz, c_send.at[m, j * far + zz], core_peer)
+
+    def along(m, side, hop):
+        held = z - side * (hop - 1)
+        there = (held >= 0) & (held < far) & (z + side >= 0) & (z + side < far)
+        return there, move(m, c, y, held, z_send.at[m, (side + 1) // 2 * far + hop], device(c, y, z + side))
 
     def gather_start(m):
         rows[m, span(c, y, z)] = x_ref[m]
-        for k in range(1, far):
-            start(m, move(m, c, y, z, z_send.at[m, k], far_peers[k]))
-        to_near(m, 0)
-        to_core(m, 0, 0)
-
-    def gather_far(m):
-        for k in range(1, far):
-            arrived(m, c, y, flipped(z, k))
-            to_near(m, k)
-            to_core(m, 0, k)
-
-    def gather_near(m):
-        for k in range(far):
-            for j in range(1, near):
-                arrived(m, c, flipped(y, j), flipped(z, k))
-                to_core(m, j, k)
+        for side in (1, -1):
+            there, copy = along(m, side, 1)
+            pl.when(there)(copy.start)
+        for copy in to_near(m, z):
+            copy.start()
+        to_core(m, 0, z).start()
+
+    def gather_far(m, hop):
+        for side in (1, -1):
+            zz = z - side * hop
+
+            @pl.when((zz >= 0) & (zz < far))
+            def _():
+                arrived(m, c, y, zz)
+                for copy in to_near(m, zz):
+                    copy.start()
+                if hop + 1 < far:
+                    there, copy = along(m, side, hop + 1)
+                    pl.when(there)(copy.start)
+                to_core(m, 0, zz).start()
+
+    def gather_near(m, hop):
+        for side in (1, -1)[: 2 if hop else 1]:
+            zz = z - side * hop
+
+            @pl.when((zz >= 0) & (zz < far))
+            def _():
+                for j in range(1, near):
+                    arrived(m, c, flipped(y, j), zz)
+                    to_core(m, j, zz).start()
 
     def gather_core(m):
-        for k in range(far):
+        for yy in range(near):
+            for zz in range(far):
+                arrived(m, 1 - c, yy, zz)
+        for side in (1, -1):
+            for hop in range(1, far):
+                there, copy = along(m, side, hop)
+                pl.when(there)(copy.wait_send)
+        for zz in range(far):
+            for copy in to_near(m, zz):
+                copy.wait_send()
             for j in range(near):
-                arrived(m, 1 - c, flipped(y, j), flipped(z, k))
-        for copy in sends[m]:
-            copy.wait_send()
+                to_core(m, j, zz).wait_send()
 
     unit_tile = 256 if units % 256 == 0 else units
     feature_tile = 512 if features % 512 == 0 else features
 
-    def expand(m, cc):
+    def key_product(m, cc):
         here = lane_span(cc)
         kr_ref[...] += lax.dot_general(
             rows[m, here, pl.ds(features, width - features)],
             rows[m, here, pl.ds(pl.multiple_of(window_start, LANES), window)],
             (((0,), (0,)), ((), ())), preferred_element_type=jnp.float32,
         )
+
+    def expand(m, cc, first, last):
+        here = lane_span(cc)
 
         def body(i, carry):
             tile = pl.ds(pl.multiple_of(i * unit_tile, unit_tile), unit_tile)
@@ -147,7 +168,7 @@
             hidden[:, tile] = (gate / (1.0 + jnp.exp(-gate)) * up).astype(jnp.bfloat16)
             return carry
 
-        lax.fori_loop(0, units // unit_tile, body, 0)
+        lax.fori_loop(first, last, body, 0)
 
     def contract(m, cc, add):
         here = lane_span(cc)
@@ -199,16 +220,15 @@
             for j in range(1, near):
                 near_sum(m, j, k).start()
 
-    def near_finish(m):
-        for k in far_order:
-            here = span(c, y, flipped(z, k))
-            total = rows[m, here, columns].astype(jnp.float32)
-            for j in range(1, near):
-                near_sum(m, j, k).wait_recv()
-                total = total + near_in[m, j - 1, flipped(z, k)].astype(jnp.float32)
-            rows[m, here, columns] = total.astype(jnp.bfloat16)
-            if k > 0:
-                far_sum(m, k).start()
+    def near_finish(m, k):
+        here = span(c, y, flipped(z, k))
+        total = rows[m, here, columns].astype(jnp.float32)
+        for j in range(1, near):
+            near_sum(m, j, k).wait_recv()
+            total = total + near_in[m, j - 1, flipped(z, k)].astype(jnp.float32)
+        rows[m, here, columns] = total.astype(jnp.bfloat16)
+        if k > 0:
+            far_sum(m, k).start()
 
     def far_finish(m):
         total = carried_ref[m].astype(jnp.float32) + rows[m, span(c, y, z), columns].astype(jnp.float32)
@@ -217,36 +237,63 @@
             total = total + far_in[m, k - 1].astype(jnp.float32)
         out_ref[m] = total.astype(jnp.bfloat16)
 
+    tiles = units // unit_tile
     gather_start(0)
-    gather_far(0)
+    for hop in range(1, far):
+        gather_far(0, hop)
+        gather_near(0, hop - 1)
+    if micro > 1:
+        gather_start(1)
+    gather_near(0, far - 1)
     for m in range(micro):
         later, before = m + 1 < micro, m > 0
+        if later and before:
+            gather_start(m + 1)
+        gather_core(m)
+        ahead = []
         if later:
-            gather_start(m + 1)
-        if m == 0:
-            gather_near(0)
-        gather_core(m)
+            for hop in range(1, far):
+                ahead.append([partial(gather_far, m + 1, hop), partial(gather_near, m + 1, hop - 1)])
+            ahead.append([partial(gather_near, m + 1, far - 1)])
+        behind = [[partial(near_finish, m - 1, k)] for k in far_order] if before else []
+        queues = [queue for queue in (ahead, behind) if queue]
+
+        def advance(most=1):
+            for queue in queues:
+                for _ in range(min(most, len(queue))):
+                    for piece in queue.pop(0):
+                        piece()
+
         if m == 0:
             loads[0].wait()
             loads[1].wait()
-        expand(m, 1 - c)
+        expand(m, 1 - c, 0, tiles // 2)
         if later:
-            gather_far(m + 1)
-        if before:
-            near_finish(m - 1)
+            advance()
+        expand(m, 1 - c, tiles // 2, tiles)
+        key_product(m, 1 - c)
+        if not later:
+            advance()
         if m == 0:
             loads[2].wait()
         contract(m, 1 - c, False)
         core_sum(m).start()
-        expand(m, c)
+        advance()
+        expand(m, c, 0, tiles // 2)
         if later:
-            gather_near(m + 1)
-        if before:
-            far_finish(m - 1)
+            advance()
+        expand(m, c, tiles // 2, tiles)
+        key_product(m, c)
+        if not later:
+            advance()
         core_sum(m).wait_recv()
         contract(m, c, True)
         near_start(m)
-    near_finish(micro - 1)
+        advance(far)
+        if before:
+            far_finish(m - 1)
+    for k in far_order:
+        near_finish(micro - 1, k)
     far_finish(micro - 1)
     for m in range(micro):
         core_sum(m).wait_send()
@@ -285,7 +332,7 @@
             pltpu.VMEM((micro, near - 1, far, tokens, features), bf16),
             pltpu.VMEM((micro, far - 1, tokens, features), bf16),
             dma((3,)),
-            dma((micro, far)),
+            dma((micro, 2 * far)),
             dma((micro, near * far)),
             dma((micro, near * far)),
             dma((micro, count)),

time: 266 us -> 229 us (0.86)
  Pallas kernels: 245 us -> 209 us
    pallas_call x2, Pallas kernels: 245 us -> 209 us  [run_layer(): pl.pallas_call(partial(layer_kernel, count, far, near, window), out_shape...]
where the time goes in v2:
time: 229 us
  Pallas kernels  209 us (91%)
  other arithmetic  9.48 us (4%)
  waiting for transfers between devices  7.22 us (3%)
    pallas_call x2, Pallas kernels, run_layer(): pl.pallas_call(partial(layer_kernel, count, far, near, window), out_shape...  209 us
    ppermute x1, waiting for transfers between devices, on_device(): lax.ppermute(output, 'pipe', [(turn, turn + 1), (sections - 1 - turn, sec...  7.22 us
  transfers between devices with their start and end apart: 1, of which 1 were waited for; matrix products, arithmetic and copies ran while one was open for 0% of the time, Pallas kernels for 0%

profile of v2, /device:TPU:0, one launch (start us, length us, event | category | flops | bytes accessed | tf_op | source)
XLA Modules:
  0.0 228.5 jit_solution(17285670083742112045)
XLA Ops:
  0.6 0.7 select_reduce_fusion
  1.4 0.1 copy.26
  1.5 0.7 select_reduce_fusion.1
  2.2 0.1 copy.23
  2.3 0.1 copy.24
  2.4 0.1 copy.27
  2.5 0.7 slice_bitcast_fusion.1
  3.2 1.3 fusion
  4.5 0.0 copy-start.1
  4.5 0.8 reduce
  5.3 0.2 fusion.2
  5.5 0.1 select_select_fusion.1
  5.6 0.8 pad_maximum_fusion.x_ref
  6.4 0.0 copy-done.1
  6.4 103.3 %shard_map.130 = (bf16[2,32,3584]{2,1,0:T(8,128)(2,1)}, f32[128,384]{1,0:T(8,128)}) custom-call(bf16[2,32,3712]{2,1,0:T(8,128)(2,1)} %pad_maximum_fusion.x_ref, bf16[2,32,3584]{2,1,0:T(8,128)(2,1)} %copy-done.1, bf16[3584,1024]{1,0:T(8,128)(2,1)} %bitcast.23, bf16[3584,1024]{1,0:T(8,128)(2,1)} %bitcast.25, bf16[1024,3584]{1,0:T(8,128)(2,1)} %bitcast.27), custom_call_target="tpu_custom_call" | custom-call | flops 22548578304 | bytes 22020096 | tf_op jit(solution)/shard_map/pallas_call | solution.py:317
  109.7 1.5 collective-permute-start
  111.2 7.2 %collective-permute-done.carried_ref = bf16[2,32,3584]{2,1,0:T(8,128)(2,1)S(1)} collective-permute-done((bf16[2,32,3584]{2,1,0:T(8,128)(2,1)}, bf16[2,32,3584]{2,1,0:T(8,128)(2,1)S(1)}, u32[]{:S(2)}, u32[]{:S(2)}) %collective-permute-start) | collective-permute-done | bytes 458784 | tf_op jit(solution)/shard_map/ppermute | solution.py:410
  118.4 0.0 copy-start
  118.5 0.2 fusion.3
  118.6 0.2 fusion.5
  118.8 0.8 pad_maximum_fusion.1.x_ref
  119.6 0.0 copy-done
  119.6 0.0 copy-start.2
  119.6 105.2 %shard_map.131 = (bf16[2,32,3584]{2,1,0:T(8,128)(2,1)}, f32[128,384]{1,0:T(8,128)}) custom-call(bf16[2,32,3712]{2,1,0:T(8,128)(2,1)} %pad_maximum_fusion.1.x_ref, bf16[2,32,3584]{2,1,0:T(8,128)(2,1)} %copy-done, bf16[3584,1024]{1,0:T(8,128)(2,1)} %bitcast.24, bf16[3584,1024]{1,0:T(8,128)(2,1)} %bitcast.26, bf16[1024,3584]{1,0:T(8,128)(2,1)} %bitcast.28), custom_call_target="tpu_custom_call" | custom-call | flops 22548578304 | bytes 22020096 | tf_op jit(solution)/shard_map/pallas_call | solution.py:317
  224.9 0.0 copy-done.2
  224.9 2.0 select_bitcast_fusion
  226.9 1.7 fusion.6
  (5 shorter events, 0.0 us)
Async XLA Ops:
  4.5 1.9 copy-start.1
  109.7 8.8 %collective-permute-start = (bf16[2,32,3584]{2,1,0:T(8,128)(2,1)}, bf16[2,32,3584]{2,1,0:T(8,128)(2,1)S(1)}, u32[]{:S(2)}, u32[]{:S(2)}) collective-permute-start(bf16[2,32,3584]{2,1,0:T(8,128)(2,1)} %get-tuple-element.7), channel_id=1, source_target_pairs={{0,16},{16,0},{1,17},{17,1},{2,18},{18,2},{3,19},{19,3},{4,20},{20... | collective-permute-start | bytes 1376264 | tf_op jit(solution)/shard_map/ppermute | solution.py:410
  118.4 1.2 copy-start
  119.6 105.2 %copy-start.2 = (bf16[2,32,3584]{2,1,0:T(8,128)(2,1)S(1)}, bf16[2,32,3584]{2,1,0:T(8,128)(2,1)}, u32[]{:S(2)}) copy-start(bf16[2,32,3584]{2,1,0:T(8,128)(2,1)} %get-tuple-element.7) | copy-start | bytes 1376260

commit v3 on v2

--- a/solution.py
+++ b/solution.py
@@ -29,14 +29,15 @@
 
 
 def layer_kernel(
-    count, far, near, window,
-    x_ref, carried_ref, gate_hbm, up_hbm, down_hbm,
+    count, far, near, window, turns,
+    tokens_ref, side_ref, gain_ref, gate_hbm, up_hbm, down_hbm,
     out_ref, kr_ref,
-    rows, w_gate, w_up, w_down, hidden, core_in, near_in, far_in,
+    rows, passed, w_gate, w_up, w_down, hidden, core_in, near_in, far_in,
     w_sem, z_send, y_send, c_send, ag_recv,
-    rc_send, rc_recv, ry_send, ry_recv, rz_send, rz_recv,
+    rc_send, rc_recv, ry_send, ry_recv, rz_send, rz_recv, p_send, p_recv,
 ):
-    micro, tokens, width = x_ref.shape
+    micro, tokens, _ = tokens_ref.shape
+    width = rows.shape[2]
     features, units = w_gate.shape
     lane_rows = near * far * tokens
     me = lax.axis_index("expert")
@@ -61,6 +62,8 @@
     near_peers = {k: device(c, flipped(y, k), z) for k in range(1, near)}
     far_peers = {k: device(c, y, flipped(z, k)) for k in range(1, far)}
     partners = [core_peer] + list(near_peers.values()) + list(far_peers.values())
+    if turns > 1:
+        partners.append((1 - pipe, me))
 
     loads = [
         pltpu.make_async_copy(gate_hbm, w_gate, w_sem.at[0]),
@@ -99,8 +102,23 @@
         there = (held >= 0) & (held < far) & (z + side >= 0) & (z + side < far)
         return there, move(m, c, y, held, z_send.at[m, (side + 1) // 2 * far + hop], device(c, y, z + side))
 
+    def pass_on(m):
+        return pltpu.make_async_remote_copy(
+            src_ref=out_ref.at[m], dst_ref=passed.at[m], send_sem=p_send.at[m],
+            recv_sem=p_recv.at[m], device_id=(1 - pipe, me), device_id_type=MESH,
+        )
+
+    def carried(m):
+        value = tokens_ref[m] if m < micro else passed[m - micro]
+        return value.astype(jnp.float32)
+
     def gather_start(m):
-        rows[m, span(c, y, z)] = x_ref[m]
+        if m >= micro:
+            pass_on(m - micro).wait_recv()
+        values = carried(m)
+        inv_rms = lax.rsqrt(jnp.mean(values * values, axis=-1, keepdims=True) + EPSILON)
+        rows[m, span(c, y, z), pl.ds(0, features)] = (values * inv_rms * gain_ref[...]).astype(jnp.bfloat16)
+        rows[m, span(c, y, z), pl.ds(features, width - features)] = side_ref[m]
         for side in (1, -1):
             there, copy = along(m, side, 1)
             pl.when(there)(copy.start)
@@ -231,13 +249,17 @@
             far_sum(m, k).start()
 
     def far_finish(m):
-        total = carried_ref[m].astype(jnp.float32) + rows[m, span(c, y, z), columns].astype(jnp.float32)
+        total = carried(m) + rows[m, span(c, y, z), columns].astype(jnp.float32)
         for k in range(1, far):
             far_sum(m, k).wait_recv()
             total = total + far_in[m, k - 1].astype(jnp.float32)
         out_ref[m] = total.astype(jnp.bfloat16)
+        if m < (turns - 1) * micro:
+            pass_on(m).start()
 
     tiles = units // unit_tile
+    tiles = units // unit_tile
+    items = turns * micro
     gather_start(0)
     for hop in range(1, far):
         gather_far(0, hop)
@@ -245,13 +267,15 @@
     if micro > 1:
         gather_start(1)
     gather_near(0, far - 1)
-    for m in range(micro):
-        later, before = m + 1 < micro, m > 0
+    for m in range(items):
+        later, before = (m + 1) % micro > 0, m % micro > 0
         if later and before:
             gather_start(m + 1)
         gather_core(m)
         ahead = []
         if later:
+            if m >= micro and not before:
+                ahead.append([partial(gather_start, m + 1)])
             for hop in range(1, far):
                 ahead.append([partial(gather_far, m + 1, hop), partial(gather_near, m + 1, hop - 1)])
             ahead.append([partial(gather_near, m + 1, far - 1)])
@@ -289,13 +313,25 @@
         core_sum(m).wait_recv()
         contract(m, c, True)
         near_start(m)
-        advance(far)
+        advance(far + 1)
         if before:
             far_finish(m - 1)
-    for k in far_order:
-        near_finish(micro - 1, k)
-    far_finish(micro - 1)
-    for m in range(micro):
+        if later:
+            continue
+        more = m + 1 < items
+        if more:
+            gather_start(m + 1)
+        for step, k in enumerate(far_order):
+            near_finish(m, k)
+            if more and step > 0:
+                gather_far(m + 1, step)
+                gather_near(m + 1, step - 1)
+        far_finish(m)
+        if more:
+            gather_near(m + 1, far - 1)
+    for m in range(items - micro):
+        pass_on(m).wait_send()
+    for m in range(items):
         core_sum(m).wait_send()
         for k in range(far):
             for j in range(1, near):
@@ -304,44 +340,49 @@
                 far_sum(m, k).wait_send()
 
 
-def run_layer(x, carried, w_gate, w_up, w_down, count):
+def run_layer(tokens_in, side, gain, w_gate, w_up, w_down, count):
     far, near = grid_of(count)
-    micro, tokens, width = x.shape
-    features, units = w_gate.shape
+    micro, tokens, features = tokens_in.shape
+    items, _, side_width = side.shape
+    units = w_gate.shape[1]
+    width = features + side_width
     lane_rows = near * far * tokens
     share = features // count
     window = -(-(share + LANES - 1) // LANES) * LANES
     bf16 = jnp.bfloat16
     dma = pltpu.SemaphoreType.DMA
-    total_rows = 2 * lane_rows * micro
+    total_rows = 2 * lane_rows * items
     return pl.pallas_call(
-        partial(layer_kernel, count, far, near, window),
+        partial(layer_kernel, count, far, near, window, items // micro),
         out_shape=(
-            jax.ShapeDtypeStruct(carried.shape, bf16),
-            jax.ShapeDtypeStruct((width - features, window), jnp.float32),
+            jax.ShapeDtypeStruct((items, tokens, features), bf16),
+            jax.ShapeDtypeStruct((side_width, window), jnp.float32),
         ),
-        in_specs=[pl.BlockSpec(memory_space=pltpu.VMEM)] * 2 + [pl.BlockSpec(memory_space=pl.ANY)] * 3,
+        in_specs=[pl.BlockSpec(memory_space=pltpu.VMEM)] * 3 + [pl.BlockSpec(memory_space=pl.ANY)] * 3,
         out_specs=(pl.BlockSpec(memory_space=pltpu.VMEM),) * 2,
         scratch_shapes=[
-            pltpu.VMEM((micro, 2 * lane_rows, width), bf16),
+            pltpu.VMEM((items, 2 * lane_rows, width), bf16),
+            pltpu.VMEM(tokens_in.shape, bf16),
             pltpu.VMEM(w_gate.shape, bf16),
             pltpu.VMEM(w_up.shape, bf16),
             pltpu.VMEM(w_down.shape, bf16),
             pltpu.VMEM((lane_rows, units), bf16),
-            pltpu.VMEM((micro, lane_rows, features), bf16),
-            pltpu.VMEM((micro, near - 1, far, tokens, features), bf16),
-            pltpu.VMEM((micro, far - 1, tokens, features), bf16),
+            pltpu.VMEM((items, lane_rows, features), bf16),
+            pltpu.VMEM((items, near - 1, far, tokens, features), bf16),
+            pltpu.VMEM((items, far - 1, tokens, features), bf16),
             dma((3,)),
-            dma((micro, 2 * far)),
-            dma((micro, near * far)),
-            dma((micro, near * far)),
-            dma((micro, count)),
+            dma((items, 2 * far)),
+            dma((items, near * far)),
+            dma((items, near * far)),
+            dma((items, count)),
+            dma((items,)),
+            dma((items,)),
+            dma((items, near - 1, far)),
+            dma((items, near - 1, far)),
+            dma((items, far - 1)),
+            dma((items, far - 1)),
             dma((micro,)),
             dma((micro,)),
-            dma((micro, near - 1, far)),
-            dma((micro, near - 1, far)),
-            dma((micro, far - 1)),
-            dma((micro, far - 1)),
         ],
         compiler_params=pltpu.CompilerParams(
             collective_id=0, has_side_effects=True, vmem_limit_bytes=60 * 1024 * 1024
@@ -351,13 +392,7 @@
             bytes_accessed=6 * features * units,
             transcendentals=total_rows * units,
         ),
-    )(x, carried, w_gate, w_up, w_down)
-
-
-def normalize(carried, norm_scale):
-    values = carried.astype(jnp.float32)
-    inv_rms = lax.rsqrt(jnp.mean(values * values, axis=-1, keepdims=True) + EPSILON)
-    return (values * inv_rms * norm_scale).astype(jnp.bfloat16)
+    )(tokens_in, side, gain, w_gate, w_up, w_down)
 
 
 def side_columns(ids, gates, tangents, count, width):
@@ -396,16 +431,21 @@
     down_states = jnp.zeros_like(down_tokens)
     up_states = jnp.zeros_like(up_tokens)
     key_grad = 0.0
-    for turn in range(sections):
-        down_on = section == turn
-        up_on = section == sections - 1 - turn
-        side = jnp.where(down_on, side_down, side_up)
-        side = jnp.where(down_on | up_on, side, jnp.zeros_like(side))
-        x = jnp.concatenate([normalize(carried, norm_gain[0]), side], axis=-1)
-        output, grad = run_layer(x, carried, w_gate[0, 0], w_up[0, 0], w_down[0, 0], count)
+    micro = down_tokens.shape[0]
+    turns = sections if sections == 2 and micro > 1 else 1
+    for call in range(0, sections, turns):
+        sides = []
+        for turn in range(call, call + turns):
+            down_on, up_on = section == turn, section == sections - 1 - turn
+            side = jnp.where(down_on, side_down, side_up)
+            sides.append(jnp.where(down_on | up_on, side, jnp.zeros_like(side)))
+        side = jnp.concatenate(sides, axis=0)
+        outputs, grad = run_layer(carried, side, norm_gain, w_gate[0, 0], w_up[0, 0], w_down[0, 0], count)
         key_grad = key_grad + grad
-        down_states = jnp.where(down_on, output, down_states)
-        up_states = jnp.where(up_on, output, up_states)
+        for turn in range(call, call + turns):
+            output = outputs[(turn - call) * micro : (turn - call + 1) * micro]
+            down_states = jnp.where(section == turn, output, down_states)
+            up_states = jnp.where(section == sections - 1 - turn, output, up_states)
         if turn + 1 < sections:
             carried = lax.ppermute(
                 output, "pipe", [(turn, turn + 1), (sections - 1 - turn, sections - 2 - turn)]

time: 229 us -> 232 us (1.013)
  Pallas kernels: 209 us -> 222 us
  waiting for transfers between devices: 7.22 us -> 0 us
  other arithmetic: 9.48 us -> 6.19 us
    pallas_call x2 -> x1, Pallas kernels: 209 us -> 222 us  [run_layer(): pl.pallas_call(partial(layer_kernel, count, far, near, window, items // m...]
    ppermute x1 -> x0, waiting for transfers between devices: 7.22 us -> none  [on_device(): lax.ppermute(output, 'pipe', [(turn, turn + 1), (sections - 1 - turn, sec...]
  transfers between devices with their start and end apart: 1 -> 0, of which waited for: 1 -> 0; matrix products, arithmetic and copies ran while one was open for 0% -> 0% of each run, Pallas kernels for 0% -> 0%
where the time goes in v3:
time: 232 us
  Pallas kernels  222 us (96%)
  other arithmetic  6.19 us (3%)
  local copies, waits for them, and re-layouts  2.68 us (1%)
    pallas_call x1, Pallas kernels, run_layer(): pl.pallas_call(partial(layer_kernel, count, far, near, window, items // m...  222 us

profile of v3, /device:TPU:0, one launch (start us, length us, event | category | flops | bytes accessed | tf_op | source)
XLA Modules:
  0.0 231.7 jit_solution(9089617696337266382)
XLA Ops:
  0.7 0.7 select_reduce_fusion.1
  1.4 0.1 copy.24
  1.5 0.7 select_reduce_fusion
  2.3 0.1 copy.27
  2.4 0.1 copy.26
  2.4 0.1 copy.23
  2.5 0.7 slice_bitcast_fusion.1
  3.3 0.1 select_select_fusion.1
  3.4 0.6 pad_maximum_fusion.side_ref
  4.0 1.8 broadcast_select_fusion.tokens_ref
  5.8 222.1 %shard_map.130 = (bf16[4,32,3584]{2,1,0:T(8,128)(2,1)}, f32[128,384]{1,0:T(8,128)}) custom-call(bf16[2,32,3584]{2,1,0:T(8,128)(2,1)} %broadcast_select_fusion.tokens_ref, bf16[4,32,128]{2,1,0:T(8,128)(2,1)} %pad_maximum_fusion.side_ref, f32[1,3584]{1,0:T(1,128)} %gain_ref.1, bf16[3584,1024]{1,0:T(8,128)(2,1)} %bitcast.23, bf16[3584,1024]{1,0:T(8,128)(2,1)} %bitcast.24, ...), custom_call_target="tpu_custom_call" | custom-call | flops 45097156608 | bytes 22020096 | tf_op jit(solution)/shard_map/pallas_call | solution.py:355
  227.9 2.1 select_bitcast_fusion
  230.1 1.6 dynamic-slice_bitcast_fusion
  (3 shorter events, 0.0 us)

commit v4 on v3

--- a/solution.py
+++ b/solution.py
@@ -319,10 +319,10 @@
         if later:
             continue
         more = m + 1 < items
-        if more:
-            gather_start(m + 1)
         for step, k in enumerate(far_order):
             near_finish(m, k)
+            if more and step == 0:
+                gather_start(m + 1)
             if more and step > 0:
                 gather_far(m + 1, step)
                 gather_near(m + 1, step - 1)

time: 232 us -> 238 us (1.026)
  Pallas kernels: 222 us -> 228 us
    pallas_call x1, Pallas kernels: 222 us -> 228 us  [run_layer(): pl.pallas_call(partial(layer_kernel, count, far, near, window, items // m...]
where the time goes in v4:
time: 238 us; the launch traced here: 237 us
  Pallas kernels  228 us (96%)
  other arithmetic  6.19 us (3%)
  local copies, waits for them, and re-layouts  2.68 us (1%)
    pallas_call x1, Pallas kernels, run_layer(): pl.pallas_call(partial(layer_kernel, count, far, near, window, items // m...  228 us

profile of v4, /device:TPU:0, one launch (start us, length us, event | category | flops | bytes accessed | tf_op | source)
XLA Modules:
  0.0 237.3 jit_solution(2697772274911009268)
XLA Ops:
  0.7 0.7 select_reduce_fusion.1
  1.4 0.1 copy.24
  1.5 0.7 select_reduce_fusion
  2.3 0.1 copy.27
  2.4 0.1 copy.26
  2.4 0.1 copy.23
  2.5 0.7 slice_bitcast_fusion.1
  3.3 0.1 select_select_fusion.1
  3.4 0.6 pad_maximum_fusion.side_ref
  4.0 1.8 broadcast_select_fusion.tokens_ref
  5.8 227.7 %shard_map.130 = (bf16[4,32,3584]{2,1,0:T(8,128)(2,1)}, f32[128,384]{1,0:T(8,128)}) custom-call(bf16[2,32,3584]{2,1,0:T(8,128)(2,1)} %broadcast_select_fusion.tokens_ref, bf16[4,32,128]{2,1,0:T(8,128)(2,1)} %pad_maximum_fusion.side_ref, f32[1,3584]{1,0:T(1,128)} %gain_ref.1, bf16[3584,1024]{1,0:T(8,128)(2,1)} %bitcast.23, bf16[3584,1024]{1,0:T(8,128)(2,1)} %bitcast.24, ...), custom_call_target="tpu_custom_call" | custom-call | flops 45097156608 | bytes 22020096 | tf_op jit(solution)/shard_map/pallas_call | solution.py:355
  233.5 2.1 select_bitcast_fusion
  235.6 1.6 dynamic-slice_bitcast_fusion
  (3 shorter events, 0.0 us)
